TPU v7x, 32 devices: a whole 2x2x4 slice. The times are simulated.
32 devices in a mesh: parts: 1, ctx: 4 (over z), pb: 4 (over y, x), row: 2 (over core).
Axes of the slice: x: 2, y: 2, z: 4, core: 2. Of those that a mesh axis runs over, the one named last changes fastest.
Arguments:
- queries: bfloat16 [2048, 3072], P(('parts', 'ctx', 'pb', 'row')), may hold values from -10 to 10
- cache_keys: bfloat16 [4096, 192], P(('parts', 'ctx')), may hold values from -10 to 10
- cache_values: bfloat16 [4096, 128], P(('parts', 'ctx')), may hold values from -6 to 6
- span_keys: bfloat16 [2048, 192], P(('parts', 'ctx')), may hold values from -10 to 10
- span_values: bfloat16 [2048, 128], P(('parts', 'ctx')), may hold values from -6 to 6
- pool_keys: float32 [32, 192], replicated, may hold values from 0.2 to 0.6
- pool_values: float32 [32, 128], replicated, may hold values from 0.05 to 0.3
- gate_logits: bfloat16 [2048, 48], P(('parts', 'ctx', 'pb', 'row')), may hold values from -6 to 6
- chosen_blocks: int32 [32, 16], P(('parts', 'ctx', 'pb', 'row')), may hold values from 0 to 95, as said below
- valid_counts: int32 [32], P(('parts', 'ctx', 'pb', 'row')), may hold values from 4 to 16
Outputs:
- mixed: bfloat16 [2048, 2048], P(('parts', 'ctx', 'pb', 'row'))
Inputs may be any that keep to these rules, and one draw needn't show every extreme that they name: `chosen_blocks`: slot 0 of tile t holds the tile's own block 64 + t. Slot s > 0 holds a block of the cache stored by ctx index (c + s) mod (4), where c is the ctx index that holds tile t; the blocks of one tile are distinct. Slots at or beyond the tile's valid count hold blocks too and are ignored.
All inputs are finite; a program needn't handle non-finite values.
Results may differ from a plain program's by a relative error of at most 0.0034.
The roundings to bfloat16 on the way count: a program that leaves them out, or rounds other values in their place, can miss the bound.
Values may be sent and summed in bfloat16 or wider, within the bound.
A program may use at most 64 MiB of HBM per device.

v0:
```python
import math
import jax
import jax.numpy as jnp
from jax import lax
from jax.sharding import PartitionSpec as P

HEADS = 16
CLEN = 32
STRIDE = 16
BLOCK = 64
WINDOW = 256
NEG_FILL = -1e30


def from_behind(value, axis, steps):
    count = lax.axis_size(axis)
    pairs = [(source, (source + steps) % count) for source in range(count)]
    return lax.ppermute(value, axis, pairs)


def pool_blocks(rows, extra, weights, stride):
    joined = jnp.concatenate([rows, extra], axis=0).astype(jnp.float32)
    blocks = rows.shape[0] // stride
    grouped = joined.reshape(blocks + 1, stride, rows.shape[1])
    leading = jnp.sum(grouped[:-1] * weights[None, :stride, :], axis=1)
    trailing = jnp.sum(grouped[1:] * weights[None, stride:, :], axis=1)
    return (leading + trailing).astype(jnp.bfloat16)


def attend(query_rows, keys, values, visible, score_scale):
    scores = jnp.dot(query_rows, keys.T, preferred_element_type=jnp.float32) * score_scale
    scores = jnp.where(visible, scores, NEG_FILL)
    highest = jnp.max(scores, axis=1, keepdims=True)
    exponent = jnp.where(visible, jnp.exp(scores - highest), 0.0)
    weights = exponent.astype(jnp.bfloat16)
    numerator = jnp.dot(weights, values, preferred_element_type=jnp.float32)
    return numerator / jnp.sum(exponent, axis=1, keepdims=True)


def local(
    queries,
    cache_keys,
    cache_values,
    span_keys,
    span_values,
    pool_keys,
    pool_values,
    gate_logits,
    chosen_blocks,
    valid_counts,
):
    owners = lax.axis_size("ctx")
    ctx_place = lax.axis_index("ctx")
    tile_place = lax.axis_index("pb") * lax.axis_size("row") + lax.axis_index("row")
    cache_len, key_width = cache_keys.shape
    value_width = cache_values.shape[1]
    span_len = span_keys.shape[0]
    tokens = queries.shape[0]
    tiles_here = chosen_blocks.shape[0]
    score_scale = 1.0 / math.sqrt(key_width)
    context_start = cache_len * owners
    local_start = tile_place * tokens
    first_pos = context_start + ctx_place * span_len + local_start
    row_count = tokens * HEADS
    query_rows = queries.reshape(row_count, key_width)
    row_pos = first_pos + jnp.arange(row_count, dtype=jnp.int32) // HEADS
    leader = ctx_place == 0
    outgoing = (
        jnp.where(leader, span_keys[:STRIDE], cache_keys[:STRIDE]),
        jnp.where(leader, span_values[:STRIDE], cache_values[:STRIDE]),
        span_keys[:STRIDE],
        span_values[:STRIDE],
    )
    heads_next = from_behind((outgoing[0], outgoing[1], outgoing[2], outgoing[3]), "ctx", -1)
    summary_keys = jnp.concatenate(
        [
            pool_blocks(cache_keys, heads_next[0], pool_keys, STRIDE),
            pool_blocks(span_keys, heads_next[2], pool_keys, STRIDE),
        ],
        axis=0,
    )
    summary_values = jnp.concatenate(
        [
            pool_blocks(cache_values, heads_next[1], pool_values, STRIDE),
            pool_blocks(span_values, heads_next[3], pool_values, STRIDE),
        ],
        axis=0,
    )
    cache_blocks = cache_len // STRIDE
    span_blocks = span_len // STRIDE
    per_ctx = cache_blocks + span_blocks
    first_row = jnp.int32(0)
    running_max = jnp.full((row_count,), NEG_FILL, jnp.float32)
    running_sum = jnp.zeros((row_count,), jnp.float32)
    running_out = jnp.zeros((row_count, value_width), jnp.float32)
    part_keys = lax.all_gather(summary_keys, "ctx", axis=0, tiled=True)
    part_values = lax.all_gather(summary_values, "ctx", axis=0, tiled=True)
    length = part_keys.shape[0]
    for lower_row in range(0, length, 512):
        upper_row = min(lower_row + 512, length)
        block_index = first_row + lower_row + jnp.arange(upper_row - lower_row, dtype=jnp.int32)
        owner_of = block_index // per_ctx
        within = block_index % per_ctx
        block_id = jnp.where(
            within < cache_blocks,
            owner_of * cache_blocks + within,
            owners * cache_blocks + owner_of * span_blocks + within - cache_blocks,
        )
        visible = (block_id * STRIDE + CLEN)[None, :] <= row_pos[:, None] + 1
        scores = (
            jnp.dot(
                query_rows, part_keys[lower_row:upper_row].T, preferred_element_type=jnp.float32
            )
            * score_scale
        )
        scores = jnp.where(visible, scores, NEG_FILL)
        new_max = jnp.maximum(running_max, jnp.max(scores, axis=1))
        exponent = jnp.where(visible, jnp.exp(scores - new_max[:, None]), 0.0)
        fading = jnp.exp(running_max - new_max)
        running_sum = running_sum * fading + jnp.sum(exponent, axis=1)
        running_out = running_out * fading[:, None] + jnp.dot(
            exponent.astype(jnp.bfloat16),
            part_values[lower_row:upper_row],
            preferred_element_type=jnp.float32,
        )
        running_max = new_max
    summary_out = running_out / running_sum[:, None]
    reach = chosen_blocks.shape[1] // owners
    arranged = chosen_blocks.reshape(tiles_here, reach, owners)
    column_of = (jnp.arange(owners, dtype=jnp.int32) - ctx_place) % owners
    requested = jnp.take(arranged, column_of, axis=2)
    wanted = lax.all_to_all(requested, "ctx", split_axis=2, concat_axis=2, tiled=True)
    cache_count = cache_len // BLOCK
    span_count = span_len // BLOCK
    from_cache = (wanted < owners * cache_count)[..., None, None]
    cache_slot = jnp.clip(wanted - ctx_place * cache_count, 0, cache_count - 1)
    span_slot = jnp.clip(wanted - owners * cache_count - ctx_place * span_count, 0, span_count - 1)
    served_keys = jnp.where(
        from_cache,
        cache_keys.reshape(cache_count, BLOCK, key_width)[cache_slot],
        span_keys.reshape(span_count, BLOCK, key_width)[span_slot],
    )
    served_values = jnp.where(
        from_cache,
        cache_values.reshape(cache_count, BLOCK, value_width)[cache_slot],
        span_values.reshape(span_count, BLOCK, value_width)[span_slot],
    )
    fetched_keys, fetched_values = (
        lax.all_to_all(served_keys, "ctx", split_axis=2, concat_axis=2, tiled=True),
        lax.all_to_all(served_values, "ctx", split_axis=2, concat_axis=2, tiled=True),
    )
    last_ctx = ctx_place == owners - 1
    tail_rows = from_behind(
        (
            jnp.where(last_ctx, cache_keys[-WINDOW:], span_keys[-WINDOW:]),
            jnp.where(last_ctx, cache_values[-WINDOW:], span_values[-WINDOW:]),
        ),
        "ctx",
        1,
    )
    reach_keys = jnp.concatenate([tail_rows[0], span_keys], axis=0)
    reach_values = jnp.concatenate([tail_rows[1], span_values], axis=0)
    gate_values = jax.nn.sigmoid(gate_logits.astype(jnp.float32)).reshape(tokens, 3, HEADS)
    offsets = jnp.arange(BLOCK, dtype=jnp.int32)
    near_offsets = jnp.arange(WINDOW + BLOCK, dtype=jnp.int32)
    slot_number = jnp.arange(reach, dtype=jnp.int32)[:, None] * owners + column_of[None, :]
    key_pos = (requested[0][:, :, None] * BLOCK + offsets).reshape(-1)
    usable = jnp.repeat((slot_number < valid_counts[0]).reshape(-1), BLOCK)
    sel_visible = usable[None, :] & (key_pos[None, :] <= row_pos[:, None])
    picked = attend(
        query_rows,
        fetched_keys[0].reshape(-1, key_width),
        fetched_values[0].reshape(-1, value_width),
        sel_visible,
        score_scale,
    )
    begin = local_start + 0
    near_keys = lax.dynamic_slice_in_dim(reach_keys, begin, WINDOW + BLOCK, 0)
    near_values = lax.dynamic_slice_in_dim(reach_values, begin, WINDOW + BLOCK, 0)
    near_pos = context_start + ctx_place * span_len - WINDOW + begin + near_offsets
    near_visible = (near_pos[None, :] <= row_pos[:, None]) & (
        near_pos[None, :] > row_pos[:, None] - WINDOW
    )
    nearby = attend(query_rows, near_keys, near_values, near_visible, score_scale)
    mixed = (
        gate_values[:, 0, :, None] * summary_out.reshape(BLOCK, HEADS, value_width)
        + gate_values[:, 1, :, None] * picked.reshape(BLOCK, HEADS, value_width)
        + gate_values[:, 2, :, None] * nearby.reshape(BLOCK, HEADS, value_width)
    )
    outputs = mixed.reshape(BLOCK, HEADS * value_width).astype(jnp.bfloat16)
    return outputs


def solution(mesh):
    return jax.shard_map(
        local,
        mesh=mesh,
        in_specs=(
            P(("parts", "ctx", "pb", "row"), None),
            P(("parts", "ctx"), None),
            P(("parts", "ctx"), None),
            P(("parts", "ctx"), None),
            P(("parts", "ctx"), None),
            P(),
            P(),
            P(("parts", "ctx", "pb", "row"), None),
            P(("parts", "ctx", "pb", "row"), None),
            P(("parts", "ctx", "pb", "row")),
        ),
        out_specs=P(("parts", "ctx", "pb", "row"), None),
        check_vma=False,
    )
```

profile of v0, /device:TPU:0, one launch (start us, length us, event | category | flops | bytes accessed | tf_op | source)
XLA Modules:
  0.0 91.8 jit_solution(5316688061465802636)
XLA Ops:
  0.0 1.3 %copy.79 = bf16[1024,192]{1,0:T(8,128)(2,1)S(1)} copy(bf16[1024,192]{0,1:T(8,128)(2,1)} %param.11) | data formatting | bytes 786432 | tf_op args[1]
  1.3 1.1 %copy.77 = bf16[512,192]{1,0:T(8,128)(2,1)S(1)} copy(bf16[512,192]{0,1:T(8,128)(2,1)} %param.13) | data formatting | bytes 393216 | tf_op args[3]
  2.4 0.6 slice_select_fusion.2
  3.0 5.1 %collective-permute-start = (bf16[16,192]{1,0:T(8,128)(2,1)}, bf16[16,192]{1,0:T(8,128)(2,1)}, u32[]{:S(2)}, u32[]{:S(2)}) collective-permute-start(bf16[16,192]{1,0:T(8,128)(2,1)} %get-tuple-element.13), channel_id=1, source_target_pairs={{0,24},{8,0},{16,8},{24,16},{1,25},{9,1},{17,9},{25,17},{2,26},{10... | collective-permute-start | bytes 18440 | tf_op jit(solution)/shard_map/ppermute | solution.py:18
  8.0 0.4 collective-permute-start.1
  8.5 1.3 %slice_select_fusion.3 = (bf16[16,128]{1,0:T(8,128)(2,1)}, bf16[16,128]{1,0:T(8,128)(2,1)}) fusion(bf16[1024,128]{1,0:T(8,128)(2,1)} %param.12, pred[]{:T(512)S(6)} %eq.10, bf16[512,128]{1,0:T(8,128)(2,1)} %param.14), kind=kLoop, calls=%fused_computation.87 | loop fusion | flops 2048 | bytes 16385 | tf_op jit(solution)/shard_map/jit(_where)/select_n | solution.py:70
  9.8 0.4 collective-permute-start.2
  10.3 0.5 broadcast.494
  10.8 1.3 %reduce.3 = s32[16]{0:T(128)S(1)} reduce(s32[1,16]{1,0:T(1,128)} %param.18, s32[]{:T(128)} %broadcast.494), dimensions={0}, to_apply=%param.18.reduce_sub_computation.3 | reduce | bytes 132 | tf_op args[8]
  12.2 0.1 copy.82
  12.3 0.6 gather_fusion
  12.9 0.1 copy.84
  13.0 0.7 copy.85
  13.7 5.3 %all-to-all-start = ((s32[1,4,4]{1,0,2:T(1,128)}), s32[1,4,4]{1,0,2:T(1,128)S(1)}, u32[]{:S(2)}, u32[]{:S(2)}) async-start(s32[1,4,4]{1,0,2:T(1,128)} %copy.85), calls=%async_computation | async-start | bytes 4096 | tf_op jit(solution)/shard_map/all_to_all | solution.py:132
  18.9 1.0 %slice_select_fusion = bf16[256,192]{0,1:T(8,128)(2,1)S(1)} fusion(bf16[512,192]{0,1:T(8,128)(2,1)} %param.13, bf16[1024,192]{0,1:T(8,128)(2,1)} %param.11, pred[]{:T(512)S(6)} %eq.11), kind=kLoop, calls=%fused_computation.60 | loop fusion | flops 49152 | bytes 294913 | tf_op jit(solution)/shard_map/jit(_where)/select_n | solution.py:155
  19.9 2.1 %collective-permute-start.4 = (bf16[256,192]{0,1:T(8,128)(2,1)S(1)}, bf16[256,192]{0,1:T(8,128)(2,1)}, u32[]{:S(2)}, u32[]{:S(2)}) collective-permute-start(bf16[256,192]{0,1:T(8,128)(2,1)S(1)} %slice_select_fusion), channel_id=1, source_target_pairs={{0,8},{8,16},{16,24},{24,0},{1,9},{9,17},{17,25},{25,1},{2,10},{10... | collective-permute-start | bytes 294920 | tf_op jit(solution)/shard_map/ppermute | solution.py:18
  22.0 0.6 multiply_add_fusion
  22.8 0.6 reshape.297
  23.4 0.1 copy.83
  24.4 0.1 lt.66
  24.5 0.6 and.99
  25.2 0.7 copy.76
  25.9 0.7 copy.81
  26.6 0.7 copy.97
  27.3 0.1 copy.89
  27.5 0.1 copy.91
  27.6 0.1 copy.86
  27.7 0.1 copy.87
  27.9 0.6 gather_fusion.1
  28.4 0.6 gather_fusion.3
  29.1 0.6 gather_fusion.2
  29.6 0.6 gather_fusion.4
  30.2 0.1 broadcast_select_fusion
  30.3 0.7 copy.95
  31.1 3.6 %all-to-all-start.2 = ((bf16[1,4,4,64,128]{4,3,1,0,2:T(8,128)(2,1)}), bf16[1,4,4,64,128]{4,3,1,0,2:T(8,128)(2,1)S(1)}, u32[]{:S(2)}, u32[]{:S(2)}) async-start(bf16[1,4,4,64,128]{4,3,1,0,2:T(8,128)(2,1)} %copy.95), calls=%async_computation.2 | async-start | bytes 524288 | tf_op jit(solution)/shard_map/all_to_all | solution.py:150
  34.7 0.9 copy_select_fusion
  35.6 2.0 %collective-permute-start.5 = (bf16[256,128]{1,0:T(8,128)(2,1)S(1)}, bf16[256,128]{1,0:T(8,128)(2,1)}, u32[]{:S(2)}, u32[]{:S(2)}) collective-permute-start(bf16[256,128]{1,0:T(8,128)(2,1)S(1)} %slice_select_fusion.1), channel_id=1, source_target_pairs={{0,8},{8,16},{16,24},{24,0},{1,9},{9,17},{17,25},{25,1},{2,10},{10... | collective-permute-start | bytes 196616 | tf_op jit(solution)/shard_map/ppermute | solution.py:18
  37.6 0.7 maximum_convert_fusion.2
  38.4 0.7 maximum_convert_fusion.3
  39.2 0.2 multiply_reduce_fusion.2
  39.4 0.1 multiply_reduce_fusion.6
  39.6 13.2 %all_gather.7 = bf16[384,128]{1,0:T(8,128)(2,1)S(1)} all-gather(bf16[96,128]{1,0:T(8,128)(2,1)S(1)} %pad_maximum_fusion.1), channel_id=1, replica_groups=mesh['parts'=1,'ctx'=4,'pb'=4,'row'=2] {'ctx'}, dimensions={0}, use_global_device_ids=true | all-gather | bytes 122880 | tf_op jit(solution)/shard_map/all_gather | solution.py:97
  52.8 0.8 maximum_convert_fusion
  53.6 0.2 fusion.53
  53.8 0.7 maximum_convert_fusion.1
  54.6 0.5 multiply_reduce_fusion
  55.2 0.3 multiply_reduce_fusion.4
  55.5 13.6 %all_gather.6 = bf16[384,192]{1,0:T(8,128)(2,1)S(1)} all-gather(bf16[96,192]{1,0:T(8,128)(2,1)S(1)} %pad_maximum_fusion), channel_id=1, replica_groups=mesh['parts'=1,'ctx'=4,'pb'=4,'row'=2] {'ctx'}, dimensions={0}, use_global_device_ids=true | all-gather | bytes 184320 | tf_op jit(solution)/shard_map/all_gather | solution.py:96
  69.0 0.4 fusion.60
  69.5 0.3 fusion.9
  69.8 0.7 fusion.5
  70.6 3.7 %all-to-all-start.1 = ((bf16[1,4,4,64,192]{4,3,1,0,2:T(8,128)(2,1)}), bf16[1,4,4,64,192]{4,3,1,0,2:T(8,128)(2,1)S(1)}, u32[]{:S(2)}, u32[]{:S(2)}) async-start(bf16[1,4,4,64,192]{4,3,1,0,2:T(8,128)(2,1)} %copy_select_fusion), calls=%async_computation.1 | async-start | bytes 1048576 | tf_op jit(solution)/shard_map/all_to_all | solution.py:149
  74.3 1.7 %fusion.59 = (f32[1024]{0:T(1024)S(1)}, f32[1024,320]{0,1:T(8,128)S(1)}) fusion(bf16[1024,192]{1,0:T(8,128)(2,1)S(1)} %reshape.297, s32[]{:T(128)S(6)} %select_n.211, bf16[256,192]{0,1:T(8,128)(2,1)} %collective-permute-done.4, bf16[512,192]{0,1:T(8,128)(2,1)S(1)} %copy-done.2, s32[1024]{0:T(1024)S(1)} %broadcast_add_fusion, s32[1024]{0:T(1024)S(1)} %fusion.31, ...), kind=kOutput, calls=%fused_computation.137 | convolution fusion | flops 128039936 | bytes 2012420 | tf_op jit(solution)/shard_map/dot_general | solution.py:31
  76.0 0.4 fusion.11
  76.4 1.5 %convolution_divide_fusion = f32[1024,128]{1,0:T(8,128)S(1)} fusion(f32[1024,320]{0,1:T(8,128)S(1)} %get-tuple-element.29, f32[1024]{0:T(1024)S(1)} %get-tuple-element.28, s32[1024]{0:T(1024)S(1)} %broadcast_add_fusion, s32[1024]{0:T(1024)S(1)} %fusion.31, s32[320]{0:T(512)S(1)} %iota_add_fusion.1, f32[1024]{0:T(1024)S(1)} %fusion.11, s32[]{:T(128)S(6)} %select_n.211, ...), kind=kOutput, calls=%fused_computation.21 | convolution fusion | flops 86147072 | bytes 2049284 | tf_op jit(solution)/shard_map/dot_general | solution.py:36
  78.0 6.4 %all-to-all-done.1 = bf16[1,4,4,64,192]{4,3,1,0,2:T(8,128)(2,1)S(1)} async-done(((bf16[1,4,4,64,192]{4,3,1,0,2:T(8,128)(2,1)}), bf16[1,4,4,64,192]{4,3,1,0,2:T(8,128)(2,1)S(1)}, u32[]{:S(2)}, u32[]{:S(2)}) %all-to-all-start.1) | async-done | bytes 393248 | tf_op jit(solution)/shard_map/all_to_all | solution.py:149
  84.4 1.2 %fusion = (f32[1024]{0:T(1024)S(1)}, f32[1024,1024]{1,0:T(8,128)S(1)}) fusion(s32[1024]{0:T(1024)S(1)} %fusion.31, s32[1024]{0:T(1024)S(1)} %add.265, pred[1024]{0:T(1024)(128)(4,1)S(1)} %copy-done.11, bf16[1024,192]{1,0:T(8,128)(2,1)S(1)} %bitcast.97, bf16[1024,192]{1,0:T(8,128)(2,1)S(1)} %reshape.297), kind=kOutput, calls=%fused_computation.8 | convolution fusion | flops 407895040 | bytes 4994048 | tf_op jit(solution)/shard_map/dot_general | solution.py:31
  85.6 1.9 %fusion.52 = f32[1024]{0:T(1024)S(1)} fusion(f32[1024]{0:T(1024)S(1)} %get-tuple-element.30, f32[1024,1024]{1,0:T(8,128)S(1)} %get-tuple-element.31, s32[1024]{0:T(1024)S(1)} %fusion.31, s32[1024]{0:T(1024)S(1)} %add.265, pred[1024]{0:T(1024)(128)(4,1)S(1)} %copy-done.11), kind=kLoop, calls=%fused_computation.130 | loop fusion | flops 7339008 | bytes 4211712 | tf_op jit(solution)/shard_map/reduce_sum | solution.py:37
  87.5 1.8 %fusion.6 = f32[1024,128]{1,0:T(8,128)S(1)} fusion(bf16[1024,128]{1,0:T(8,128)(2,1)S(1)} %bitcast.98, f32[1024]{0:T(1024)S(1)} %fusion.52, f32[1024,1024]{1,0:T(8,128)S(1)} %get-tuple-element.31, f32[1024]{0:T(1024)S(1)} %get-tuple-element.30, s32[1024]{0:T(1024)S(1)} %fusion.31, s32[1024]{0:T(1024)S(1)} %add.265, pred[1024]{0:T(1024)(128)(4,1)S(1)} %copy-done.11), kind=kOutput, calls=%fused_computation.20 | convolution fusion | flops 275906560 | bytes 4998144 | tf_op jit(solution)/shard_map/dot_general | solution.py:36
  89.5 0.2 mul.192
  89.7 0.4 copy-done.5
  90.2 0.2 mul.223
  90.4 0.2 mul.234
  90.6 1.3 %fusion.25 = bf16[64,2048]{1,0:T(8,128)(2,1)} fusion(f32[64,2048]{1,0:T(8,128)S(1)} %reshape.305, f32[8,8,16,128]{3,2,1,0:T(8,128)S(1)} %bitcast.92, f32[64,2048]{1,0:T(8,128)S(1)} %reshape.304, f32[8,8,16,128]{3,2,1,0:T(8,128)S(1)} %bitcast.91, f32[64,2048]{1,0:T(8,128)S(1)} %reshape.298, f32[8,8,16,128]{3,2,1,0:T(8,128)S(1)} %bitcast.90), kind=kLoop, calls=%fused_computation.40 | loop fusion | flops 786432 | bytes 3407872 | tf_op jit(solution)/shard_map/convert_element_type | solution.py:190
  (75 shorter events, 1.4 us)
Async XLA Ops:
  0.0 22.7 %copy-start.1 = (bf16[1024,128]{1,0:T(8,128)(2,1)S(1)}, bf16[1024,128]{1,0:T(8,128)(2,1)}, u32[]{:S(2)}) copy-start(bf16[1024,128]{1,0:T(8,128)(2,1)} %param.12) | copy-start | bytes 786436
  0.0 22.7 %copy-start = (bf16[512,128]{1,0:T(8,128)(2,1)S(1)}, bf16[512,128]{1,0:T(8,128)(2,1)}, u32[]{:S(2)}) copy-start(bf16[512,128]{1,0:T(8,128)(2,1)} %param.14) | copy-start | bytes 393220
  0.0 22.7 %copy-start.7 = (f32[32,192]{1,0:T(8,128)S(1)}, f32[32,192]{1,0:T(8,128)}, u32[]{:S(2)}) copy-start(f32[32,192]{1,0:T(8,128)} %param.15) | copy-start | bytes 73732
  0.0 22.7 %copy-start.3 = (bf16[64,3072]{1,0:T(8,128)(2,1)S(1)}, bf16[64,3072]{1,0:T(8,128)(2,1)}, u32[]{:S(2)}) copy-start(bf16[64,3072]{1,0:T(8,128)(2,1)} %param.10) | copy-start | bytes 1179652
  0.0 23.4 %copy-start.8 = (f32[32,128]{1,0:T(8,128)S(1)}, f32[32,128]{1,0:T(8,128)}, u32[]{:S(2)}) copy-start(f32[32,128]{1,0:T(8,128)} %param.16) | copy-start | bytes 49156
  0.0 25.2 %copy-start.9 = (bf16[64,48]{0,1:T(8,128)(2,1)S(1)}, bf16[64,48]{0,1:T(8,128)(2,1)}, u32[]{:S(2)}) copy-start(bf16[64,48]{0,1:T(8,128)(2,1)} %param.17) | copy-start | bytes 18436
  3.0 49.8 %collective-permute-start = (bf16[16,192]{1,0:T(8,128)(2,1)}, bf16[16,192]{1,0:T(8,128)(2,1)}, u32[]{:S(2)}, u32[]{:S(2)}) collective-permute-start(bf16[16,192]{1,0:T(8,128)(2,1)} %get-tuple-element.13), channel_id=1, source_target_pairs={{0,24},{8,0},{16,8},{24,16},{1,25},{9,1},{17,9},{25,17},{2,26},{10... | collective-permute-start | bytes 18440 | tf_op jit(solution)/shard_map/ppermute | solution.py:18
  8.0 45.7 %collective-permute-start.1 = (bf16[16,192]{1,0:T(8,128)(2,1)}, bf16[16,192]{1,0:T(8,128)(2,1)}, u32[]{:S(2)}, u32[]{:S(2)}) collective-permute-start(bf16[16,192]{1,0:T(8,128)(2,1)} %get-tuple-element.14), channel_id=1, source_target_pairs={{0,24},{8,0},{16,8},{24,16},{1,25},{9,1},{17,9},{25,17},{2,26},{10... | collective-permute-start | bytes 18440 | tf_op jit(solution)/shard_map/ppermute | solution.py:18
  9.8 25.8 %collective-permute-start.2 = (bf16[16,128]{1,0:T(8,128)(2,1)}, bf16[16,128]{1,0:T(8,128)(2,1)}, u32[]{:S(2)}, u32[]{:S(2)}) collective-permute-start(bf16[16,128]{1,0:T(8,128)(2,1)} %get-tuple-element.15), channel_id=1, source_target_pairs={{0,24},{8,0},{16,8},{24,16},{1,25},{9,1},{17,9},{25,17},{2,26},{10... | collective-permute-start | bytes 12296 | tf_op jit(solution)/shard_map/ppermute | solution.py:18
  10.2 28.2 %collective-permute-start.3 = (bf16[16,128]{1,0:T(8,128)(2,1)}, bf16[16,128]{1,0:T(8,128)(2,1)}, u32[]{:S(2)}, u32[]{:S(2)}) collective-permute-start(bf16[16,128]{1,0:T(8,128)(2,1)} %get-tuple-element.16), channel_id=1, source_target_pairs={{0,24},{8,0},{16,8},{24,16},{1,25},{9,1},{17,9},{25,17},{2,26},{10... | collective-permute-start | bytes 12296 | tf_op jit(solution)/shard_map/ppermute | solution.py:18
  13.7 13.6 %all-to-all-start = ((s32[1,4,4]{1,0,2:T(1,128)}), s32[1,4,4]{1,0,2:T(1,128)S(1)}, u32[]{:S(2)}, u32[]{:S(2)}) async-start(s32[1,4,4]{1,0,2:T(1,128)} %copy.85), calls=%async_computation | async-start | bytes 4096 | tf_op jit(solution)/shard_map/all_to_all | solution.py:132
  19.9 54.4 %collective-permute-start.4 = (bf16[256,192]{0,1:T(8,128)(2,1)S(1)}, bf16[256,192]{0,1:T(8,128)(2,1)}, u32[]{:S(2)}, u32[]{:S(2)}) collective-permute-start(bf16[256,192]{0,1:T(8,128)(2,1)S(1)} %slice_select_fusion), channel_id=1, source_target_pairs={{0,8},{8,16},{16,24},{24,0},{1,9},{9,17},{17,25},{25,1},{2,10},{10... | collective-permute-start | bytes 294920 | tf_op jit(solution)/shard_map/ppermute | solution.py:18
  31.1 39.6 %all-to-all-start.2 = ((bf16[1,4,4,64,128]{4,3,1,0,2:T(8,128)(2,1)}), bf16[1,4,4,64,128]{4,3,1,0,2:T(8,128)(2,1)S(1)}, u32[]{:S(2)}, u32[]{:S(2)}) async-start(bf16[1,4,4,64,128]{4,3,1,0,2:T(8,128)(2,1)} %copy.95), calls=%async_computation.2 | async-start | bytes 524288 | tf_op jit(solution)/shard_map/all_to_all | solution.py:150
  35.6 40.8 %collective-permute-start.5 = (bf16[256,128]{1,0:T(8,128)(2,1)S(1)}, bf16[256,128]{1,0:T(8,128)(2,1)}, u32[]{:S(2)}, u32[]{:S(2)}) collective-permute-start(bf16[256,128]{1,0:T(8,128)(2,1)S(1)} %slice_select_fusion.1), channel_id=1, source_target_pairs={{0,8},{8,16},{16,24},{24,0},{1,9},{9,17},{17,25},{25,1},{2,10},{10... | collective-permute-start | bytes 196616 | tf_op jit(solution)/shard_map/ppermute | solution.py:18
  54.6 14.4 %copy-start.10 = (s32[384]{0:T(512)S(1)}, s32[384]{0:T(512)}, u32[]{:S(2)}) copy-start(s32[384]{0:T(512)} %multiply_add_fusion) | copy-start | bytes 4612
  70.5 3.8 %copy-start.2 = (bf16[512,192]{0,1:T(8,128)(2,1)S(1)}, bf16[512,192]{0,1:T(8,128)(2,1)}, u32[]{:S(2)}) copy-start(bf16[512,192]{0,1:T(8,128)(2,1)} %param.13) | copy-start | bytes 589828
  70.6 13.7 %all-to-all-start.1 = ((bf16[1,4,4,64,192]{4,3,1,0,2:T(8,128)(2,1)}), bf16[1,4,4,64,192]{4,3,1,0,2:T(8,128)(2,1)S(1)}, u32[]{:S(2)}, u32[]{:S(2)}) async-start(bf16[1,4,4,64,192]{4,3,1,0,2:T(8,128)(2,1)} %copy_select_fusion), calls=%async_computation.1 | async-start | bytes 1048576 | tf_op jit(solution)/shard_map/all_to_all | solution.py:149
  77.9 6.5 %copy-start.11 = (pred[1024]{0:T(1024)(128)(4,1)S(1)}, pred[1024]{0:T(1024)(128)(4,1)}, u32[]{:S(2)}) copy-start(pred[1024]{0:T(1024)(128)(4,1)} %and.99) | copy-start | bytes 3076
  87.5 2.0 %copy-start.4 = (f32[64,16]{1,0:T(8,128)S(1)}, f32[64,16]{1,0:T(8,128)}, u32[]{:S(2)}) copy-start(f32[64,16]{1,0:T(8,128)} %copy.76) | copy-start | bytes 12292
  89.4 0.8 copy-start.5
  89.4 0.9 %copy-start.6 = (f32[64,16]{1,0:T(8,128)S(1)}, f32[64,16]{1,0:T(8,128)}, u32[]{:S(2)}) copy-start(f32[64,16]{1,0:T(8,128)} %copy.97) | copy-start | bytes 12292
where the time goes:
time: 92.6 us; the launch traced here: 91.8 us
  blocking collectives  26.8 us (29%)
  starting transfers between devices  22.7 us (25%)
  other arithmetic  14.1 us (15%)
  local copies, waits for them, and re-layouts  13.3 us (14%)
  matrix products  7.31 us (8%)
  waiting for transfers between devices  6.38 us (7%)
  between operations  1.25 us (1%)
    all_gather x1, blocking collectives, local(): part_keys = lax.all_gather(summary_keys, 'ctx', axis=0, tiled=True)  13.6 us
    all_gather x1, blocking collectives, local(): part_values = lax.all_gather(summary_values, 'ctx', axis=0, tiled=True)  13.2 us
    ppermute x6, starting transfers between devices, from_behind(): return lax.ppermute(value, axis, pairs)  10.1 us
    all_to_all x1, waiting for transfers between devices, local(): lax.all_to_all(served_keys, 'ctx', split_axis=2, concat_axis=2, tiled=True)  6.36 us
    all_to_all x1, starting transfers between devices, local(): lax.all_to_all(requested, 'ctx', split_axis=2, concat_axis=2, tiled=True)  5.27 us
    all_to_all x1, starting transfers between devices, local(): lax.all_to_all(served_keys, 'ctx', split_axis=2, concat_axis=2, tiled=True)  3.66 us
    all_to_all x1, starting transfers between devices, local(): lax.all_to_all(served_values, 'ctx', split_axis=2, concat_axis=2, tiled=T...  3.63 us
    unnamed x27, local copies, waits for them, and re-layouts  3.33 us
  transfers between devices with their start and end apart: 9, of which 1 were waited for; matrix products, arithmetic and copies ran while one was open for 27% of the time, Pallas kernels for 0%

commit v1 on v0

--- a/solution.py
+++ b/solution.py
@@ -10,6 +10,18 @@
 BLOCK = 64
 WINDOW = 256
 NEG_FILL = -1e30
+
+
+def rotated_exchange(x, axis, split, join):
+    ways, here = (lax.axis_size(axis), lax.axis_index(axis))
+    width = x.shape[split] // ways
+    turned = jnp.roll(x, -here * width, axis=split)
+    got = [lax.slice_in_dim(turned, 0, width, axis=split)]
+    for far in range(1, ways):
+        sent = lax.slice_in_dim(turned, far * width, (far + 1) * width, axis=split)
+        got.append(lax.ppermute(sent, axis, [(d, (d + far) % ways) for d in range(ways)]))
+    line = jnp.concatenate(got[::-1], axis=join)
+    return jnp.roll(line, (here + 1) * got[0].shape[join], axis=join)
 
 
 def from_behind(value, axis, steps):
@@ -147,7 +159,7 @@
     )
     fetched_keys, fetched_values = (
         lax.all_to_all(served_keys, "ctx", split_axis=2, concat_axis=2, tiled=True),
-        lax.all_to_all(served_values, "ctx", split_axis=2, concat_axis=2, tiled=True),
+        rotated_exchange(served_values, "ctx", 2, 2),
     )
     last_ctx = ctx_place == owners - 1
     tail_rows = from_behind(

time: 92.6 us -> 82.4 us (0.89)
  waiting for transfers between devices: 6.38 us -> 0.08 us
  other arithmetic: 14.1 us -> 10 us
  local copies, waits for them, and re-layouts: 13.3 us -> 10.2 us
  blocking collectives: 26.8 us -> 29.9 us
  starting transfers between devices: 22.7 us -> 24.1 us
  matrix products: 7.31 us -> 6.38 us
    all_to_all x1, waiting for transfers between devices: 6.36 us -> 0.01 us  [local(): lax.all_to_all(served_keys, 'ctx', split_axis=2, concat_axis=2, tiled=True)]
    ppermute x0 -> x3, starting transfers between devices: none -> 5 us  [rotated_exchange(): lax.ppermute(sent, axis, [(d, (d + far) % ways) for d in range(ways)])]
    all_to_all x1 -> x0, starting transfers between devices: 3.63 us -> none  [local(): lax.all_to_all(served_values, 'ctx', split_axis=2, concat_axis=2, tiled=T...]
    convert_element_type x4, other arithmetic: 2.93 us -> 0.17 us  [pool_blocks(): joined = jnp.concatenate([rows, extra], axis=0).astype(jnp.float32)]
    all_gather x1, blocking collectives: 13.2 us -> 15.8 us  [local(): part_values = lax.all_gather(summary_values, 'ctx', axis=0, tiled=True)]
    unnamed x27 -> x17, local copies, waits for them, and re-layouts: 3.33 us -> 3.31 us
  transfers between devices with their start and end apart: 9 -> 11, of which waited for: 1 -> 1; matrix products, arithmetic and copies ran while one was open for 27% -> 21% of each run, Pallas kernels for 0% -> 0%
where the time goes in v1:
time: 82.4 us; the launch traced here: 82 us
  blocking collectives  29.9 us (36%)
  starting transfers between devices  24.1 us (29%)
  local copies, waits for them, and re-layouts  10.2 us (12%)
  other arithmetic  10 us (12%)
  matrix products  6.38 us (8%)
  between operations  1.25 us (2%)
    all_gather x1, blocking collectives, local(): part_values = lax.all_gather(summary_values, 'ctx', axis=0, tiled=True)  15.8 us
    all_gather x1, blocking collectives, local(): part_keys = lax.all_gather(summary_keys, 'ctx', axis=0, tiled=True)  14.1 us
    ppermute x6, starting transfers between devices, from_behind(): return lax.ppermute(value, axis, pairs)  10.2 us
    all_to_all x1, starting transfers between devices, local(): lax.all_to_all(requested, 'ctx', split_axis=2, concat_axis=2, tiled=True)  5.25 us
    ppermute x3, starting transfers between devices, rotated_exchange(): lax.ppermute(sent, axis, [(d, (d + far) % ways) for d in range(ways)])  5 us
    all_to_all x1, starting transfers between devices, local(): lax.all_to_all(served_keys, 'ctx', split_axis=2, concat_axis=2, tiled=True)  3.59 us
    dot_general x2, matrix products, attend(): numerator = jnp.dot(weights, values, preferred_element_type=jnp.float32)  3.33 us
    unnamed x17, local copies, waits for them, and re-layouts  3.31 us
  transfers between devices with their start and end apart: 11, of which 1 were waited for; matrix products, arithmetic and copies ran while one was open for 21% of the time, Pallas kernels for 0%

profile of v1, /device:TPU:0, one launch (start us, length us, event | category | flops | bytes accessed | tf_op | source)
XLA Modules:
  0.0 82.0 jit_solution(17214253620957174573)
XLA Ops:
  0.0 1.3 %copy.56 = bf16[1024,192]{1,0:T(8,128)(2,1)S(1)} copy(bf16[1024,192]{0,1:T(8,128)(2,1)} %param.13) | data formatting | bytes 786432 | tf_op args[1]
  1.3 1.1 %copy.54 = bf16[512,192]{1,0:T(8,128)(2,1)S(1)} copy(bf16[512,192]{0,1:T(8,128)(2,1)} %param.15) | data formatting | bytes 393216 | tf_op args[3]
  2.4 5.1 %collective-permute-start = (bf16[16,192]{1,0:T(8,128)(2,1)S(1)}, bf16[16,192]{1,0:T(8,128)(2,1)S(1)}, u32[]{:S(2)}, u32[]{:S(2)}) collective-permute-start(bf16[16,192]{1,0:T(8,128)(2,1)S(1)} %get-tuple-element.14), channel_id=1, source_target_pairs={{0,24},{8,0},{16,8},{24,16},{1,25},{9,1},{17,9},{25,17},{2,26},{10... | collective-permute-start | bytes 18440 | tf_op jit(solution)/shard_map/ppermute | solution.py:30
  7.5 0.4 collective-permute-start.1
  8.0 0.7 slice_select_fusion.3
  8.7 0.4 collective-permute-start.2
  9.2 0.5 broadcast.495
  9.7 1.3 %reduce.3 = s32[16]{0:T(128)S(1)} reduce(s32[1,16]{1,0:T(1,128)} %param.20, s32[]{:T(128)} %broadcast.495), dimensions={0}, to_apply=%param.20.reduce_sub_computation.3 | reduce | bytes 132 | tf_op args[8]
  11.1 0.1 reshape.306
  11.1 0.1 copy.59
  11.2 0.6 gather_fusion
  11.8 0.1 copy.61
  11.9 0.7 copy.62
  12.6 5.3 %all-to-all-start = ((s32[1,4,4]{1,0,2:T(1,128)}), s32[1,4,4]{1,0,2:T(1,128)S(1)}, u32[]{:S(2)}, u32[]{:S(2)}) async-start(s32[1,4,4]{1,0,2:T(1,128)} %copy.62), calls=%async_computation | async-start | bytes 4096 | tf_op jit(solution)/shard_map/all_to_all | solution.py:144
  17.8 1.0 %slice_select_fusion = bf16[256,192]{0,1:T(8,128)(2,1)S(1)} fusion(bf16[512,192]{0,1:T(8,128)(2,1)} %param.15, bf16[1024,192]{0,1:T(8,128)(2,1)} %param.13, pred[]{:T(512)S(6)} %eq.13), kind=kLoop, calls=%fused_computation.78 | loop fusion | flops 49152 | bytes 294913 | tf_op jit(solution)/shard_map/jit(_where)/select_n | solution.py:167
  18.8 2.1 %collective-permute-start.7 = (bf16[256,192]{0,1:T(8,128)(2,1)S(1)}, bf16[256,192]{0,1:T(8,128)(2,1)S(1)}, u32[]{:S(2)}, u32[]{:S(2)}) collective-permute-start(bf16[256,192]{0,1:T(8,128)(2,1)S(1)} %slice_select_fusion), channel_id=1, source_target_pairs={{0,8},{8,16},{16,24},{24,0},{1,9},{9,17},{17,25},{25,1},{2,10},{10... | collective-permute-start | bytes 294920 | tf_op jit(solution)/shard_map/ppermute | solution.py:30
  21.1 0.6 reshape.297
  21.7 0.1 copy.60
  22.7 0.1 lt.75
  22.9 0.1 and.104
  23.0 0.1 copy.53
  23.3 0.1 copy.66
  23.4 0.1 reshape.318
  23.5 0.1 copy.68
  23.6 0.1 reshape.326
  23.7 0.1 copy.63
  23.8 0.1 copy.64
  23.9 0.6 gather_fusion.1
  24.5 0.6 gather_fusion.2
  25.1 0.9 %copy_select_fusion = bf16[1,4,4,64,192]{4,3,1,0,2:T(8,128)(2,1)} fusion(bf16[1,4,4,64,192]{4,3,2,1,0:T(8,128)(2,1)S(1)} %bitcast.89, bf16[1,4,4,64,192]{4,3,2,1,0:T(8,128)(2,1)S(1)} %bitcast.88, pred[4,4]{0,1:T(4,128)(4,1)S(1)} %copy.64), kind=kLoop, calls=%fused_computation.54 | loop fusion | flops 196608 | bytes 1179664 | tf_op jit(solution)/shard_map/jit(_where)/select_n | solution.py:150
  26.0 3.6 %all-to-all-start.1 = ((bf16[1,4,4,64,192]{4,3,1,0,2:T(8,128)(2,1)}), bf16[1,4,4,64,192]{4,3,1,0,2:T(8,128)(2,1)S(1)}, u32[]{:S(2)}, u32[]{:S(2)}) async-start(bf16[1,4,4,64,192]{4,3,1,0,2:T(8,128)(2,1)} %copy_select_fusion), calls=%async_computation.1 | async-start | bytes 1048576 | tf_op jit(solution)/shard_map/all_to_all | solution.py:161
  29.6 0.6 gather_fusion.3
  30.2 0.6 gather_fusion.4
  30.8 0.1 broadcast_select_fusion
  30.9 0.1 fusion.34
  31.0 2.1 %collective-permute-start.8 = (bf16[256,128]{1,0:T(8,128)(2,1)S(1)}, bf16[256,128]{1,0:T(8,128)(2,1)}, u32[]{:S(2)}, u32[]{:S(2)}) collective-permute-start(bf16[256,128]{1,0:T(8,128)(2,1)S(1)} %slice_select_fusion.1), channel_id=1, source_target_pairs={{0,8},{8,16},{16,24},{24,0},{1,9},{9,17},{17,25},{25,1},{2,10},{10... | collective-permute-start | bytes 196616 | tf_op jit(solution)/shard_map/ppermute | solution.py:30
  33.2 1.9 %collective-permute-start.4 = (bf16[1,4,1,64,128]{4,3,2,1,0:T(8,128)(2,1)S(1)}, bf16[1,4,1,64,128]{4,3,2,1,0:T(8,128)(2,1)S(1)}, u32[]{:S(2)}, u32[]{:S(2)}) collective-permute-start(bf16[1,4,1,64,128]{4,3,2,1,0:T(8,128)(2,1)S(1)} %get-tuple-element.19), channel_id=1, source_target_pairs={{0,24},{8,0},{16,8},{24,16},{1,25},{9,1},{17,9},{25,17},{2,26},{10... | collective-permute-start | bytes 196616 | tf_op jit(solution)/shard_map/ppermute | solution.py:22
  35.2 0.2 multiply_reduce_fusion.2
  35.4 0.1 multiply_reduce_fusion.6
  35.6 15.8 %all_gather.7 = bf16[384,128]{1,0:T(8,128)(2,1)S(1)} all-gather(bf16[96,128]{1,0:T(8,128)(2,1)S(1)} %pad_maximum_fusion.1), channel_id=1, replica_groups=mesh['parts'=1,'ctx'=4,'pb'=4,'row'=2] {'ctx'}, dimensions={0}, use_global_device_ids=true | all-gather | bytes 122880 | tf_op jit(solution)/shard_map/all_gather | solution.py:109
  51.4 0.6 collective-permute-start.5
  52.1 0.2 fusion.61
  52.3 2.5 %collective-permute-start.6 = (bf16[1,4,1,64,128]{4,3,2,1,0:T(8,128)(2,1)S(1)}, bf16[1,4,1,64,128]{4,3,2,1,0:T(8,128)(2,1)S(1)}, u32[]{:S(2)}, u32[]{:S(2)}) collective-permute-start(bf16[1,4,1,64,128]{4,3,2,1,0:T(8,128)(2,1)S(1)} %get-tuple-element.17), channel_id=1, source_target_pairs={{0,8},{8,16},{16,24},{24,0},{1,9},{9,17},{17,25},{25,1},{2,10},{10... | collective-permute-start | bytes 196616 | tf_op jit(solution)/shard_map/ppermute | solution.py:22
  54.9 0.5 multiply_reduce_fusion
  55.4 0.3 multiply_reduce_fusion.4
  55.7 14.1 %all_gather.6 = bf16[384,192]{1,0:T(8,128)(2,1)S(1)} all-gather(bf16[96,192]{1,0:T(8,128)(2,1)S(1)} %pad_maximum_fusion), channel_id=1, replica_groups=mesh['parts'=1,'ctx'=4,'pb'=4,'row'=2] {'ctx'}, dimensions={0}, use_global_device_ids=true | all-gather | bytes 184320 | tf_op jit(solution)/shard_map/all_gather | solution.py:108
  69.9 0.4 fusion.69
  70.3 0.3 fusion.9
  70.7 0.7 fusion.5
  71.3 0.1 reshape.298
  71.5 0.3 fusion.30
  71.8 0.4 copy-done.2
  72.3 0.7 fusion.68
  73.0 0.4 fusion.11
  73.4 1.5 %convolution_divide_fusion = f32[1024,128]{1,0:T(8,128)S(1)} fusion(f32[1024,320]{0,1:T(8,128)S(1)} %get-tuple-element.34, f32[1024]{0:T(1024)S(1)} %get-tuple-element.33, s32[1024]{0:T(1024)S(1)} %broadcast_add_fusion, s32[1024]{0:T(1024)S(1)} %fusion.39, s32[320]{0:T(512)S(1)} %iota_add_fusion.1, f32[1024]{0:T(1024)S(1)} %fusion.11, s32[]{:T(128)S(6)} %select_n.220, ...), kind=kOutput, calls=%fused_computation.21 | convolution fusion | flops 86147072 | bytes 2049284 | tf_op jit(solution)/shard_map/dot_general | solution.py:48
  74.9 0.1 reshape.305
  75.1 1.2 %fusion = (f32[1024]{0:T(1024)S(1)}, f32[1024,1024]{1,0:T(8,128)S(1)}) fusion(s32[1024]{0:T(1024)S(1)} %fusion.39, s32[1024]{0:T(1024)S(1)} %add.276, pred[1024]{0:T(1024)(128)(4,1)S(1)} %and.104, bf16[1024,192]{1,0:T(8,128)(2,1)S(1)} %bitcast.97, bf16[1024,192]{1,0:T(8,128)(2,1)S(1)} %reshape.297), kind=kOutput, calls=%fused_computation.8 | convolution fusion | flops 407895040 | bytes 4994048 | tf_op jit(solution)/shard_map/dot_general | solution.py:43
  76.3 1.9 %fusion.60 = f32[1024]{0:T(1024)S(1)} fusion(f32[1024]{0:T(1024)S(1)} %get-tuple-element.35, f32[1024,1024]{1,0:T(8,128)S(1)} %get-tuple-element.36, s32[1024]{0:T(1024)S(1)} %fusion.39, s32[1024]{0:T(1024)S(1)} %add.276, pred[1024]{0:T(1024)(128)(4,1)S(1)} %and.104), kind=kLoop, calls=%fused_computation.148 | loop fusion | flops 7339008 | bytes 4211712 | tf_op jit(solution)/shard_map/reduce_sum | solution.py:49
  78.2 1.8 %fusion.6 = f32[1024,128]{1,0:T(8,128)S(1)} fusion(bf16[1024,128]{1,0:T(8,128)(2,1)S(1)} %bitcast.98, f32[1024]{0:T(1024)S(1)} %fusion.60, f32[1024,1024]{1,0:T(8,128)S(1)} %get-tuple-element.36, f32[1024]{0:T(1024)S(1)} %get-tuple-element.35, s32[1024]{0:T(1024)S(1)} %fusion.39, s32[1024]{0:T(1024)S(1)} %add.276, pred[1024]{0:T(1024)(128)(4,1)S(1)} %and.104), kind=kOutput, calls=%fused_computation.20 | convolution fusion | flops 275906560 | bytes 4998144 | tf_op jit(solution)/shard_map/dot_general | solution.py:48
  80.0 0.1 reshape.304
  80.1 0.2 mul.192
  80.3 0.2 mul.223
  80.5 0.2 mul.234
  80.7 1.3 %fusion.25 = bf16[64,2048]{1,0:T(8,128)(2,1)} fusion(f32[64,2048]{1,0:T(8,128)S(1)} %reshape.305, f32[8,8,16,128]{3,2,1,0:T(8,128)S(1)} %bitcast.92, f32[64,2048]{1,0:T(8,128)S(1)} %reshape.304, f32[8,8,16,128]{3,2,1,0:T(8,128)S(1)} %bitcast.91, f32[64,2048]{1,0:T(8,128)S(1)} %reshape.298, f32[8,8,16,128]{3,2,1,0:T(8,128)S(1)} %bitcast.90), kind=kLoop, calls=%fused_computation.40 | loop fusion | flops 786432 | bytes 3407872 | tf_op jit(solution)/shard_map/convert_element_type | solution.py:202
  (70 shorter events, 1.3 us)
Async XLA Ops:
  0.0 21.0 %copy-start.1 = (bf16[1024,128]{1,0:T(8,128)(2,1)S(1)}, bf16[1024,128]{1,0:T(8,128)(2,1)}, u32[]{:S(2)}) copy-start(bf16[1024,128]{1,0:T(8,128)(2,1)} %param.14) | copy-start | bytes 786436
  0.0 21.0 %copy-start = (bf16[512,128]{1,0:T(8,128)(2,1)S(1)}, bf16[512,128]{1,0:T(8,128)(2,1)}, u32[]{:S(2)}) copy-start(bf16[512,128]{1,0:T(8,128)(2,1)} %param.16) | copy-start | bytes 393220
  0.0 21.1 %copy-start.4 = (f32[32,192]{1,0:T(8,128)S(1)}, f32[32,192]{1,0:T(8,128)}, u32[]{:S(2)}) copy-start(f32[32,192]{1,0:T(8,128)} %param.17) | copy-start | bytes 73732
  0.0 21.1 %copy-start.3 = (bf16[64,3072]{1,0:T(8,128)(2,1)S(1)}, bf16[64,3072]{1,0:T(8,128)(2,1)}, u32[]{:S(2)}) copy-start(bf16[64,3072]{1,0:T(8,128)(2,1)} %param.12) | copy-start | bytes 1179652
  0.0 21.7 %copy-start.5 = (f32[32,128]{1,0:T(8,128)S(1)}, f32[32,128]{1,0:T(8,128)}, u32[]{:S(2)}) copy-start(f32[32,128]{1,0:T(8,128)} %param.18) | copy-start | bytes 49156
  0.0 22.9 %copy-start.6 = (bf16[64,48]{0,1:T(8,128)(2,1)S(1)}, bf16[64,48]{0,1:T(8,128)(2,1)}, u32[]{:S(2)}) copy-start(bf16[64,48]{0,1:T(8,128)(2,1)} %param.19) | copy-start | bytes 18436
  2.4 49.0 %collective-permute-start = (bf16[16,192]{1,0:T(8,128)(2,1)S(1)}, bf16[16,192]{1,0:T(8,128)(2,1)S(1)}, u32[]{:S(2)}, u32[]{:S(2)}) collective-permute-start(bf16[16,192]{1,0:T(8,128)(2,1)S(1)} %get-tuple-element.14), channel_id=1, source_target_pairs={{0,24},{8,0},{16,8},{24,16},{1,25},{9,1},{17,9},{25,17},{2,26},{10... | collective-permute-start | bytes 18440 | tf_op jit(solution)/shard_map/ppermute | solution.py:30
  7.5 44.7 %collective-permute-start.1 = (bf16[16,192]{1,0:T(8,128)(2,1)S(1)}, bf16[16,192]{1,0:T(8,128)(2,1)S(1)}, u32[]{:S(2)}, u32[]{:S(2)}) collective-permute-start(bf16[16,192]{1,0:T(8,128)(2,1)S(1)} %get-tuple-element.15), channel_id=1, source_target_pairs={{0,24},{8,0},{16,8},{24,16},{1,25},{9,1},{17,9},{25,17},{2,26},{10... | collective-permute-start | bytes 18440 | tf_op jit(solution)/shard_map/ppermute | solution.py:30
  8.7 22.4 %collective-permute-start.2 = (bf16[16,128]{1,0:T(8,128)(2,1)S(1)}, bf16[16,128]{1,0:T(8,128)(2,1)S(1)}, u32[]{:S(2)}, u32[]{:S(2)}) collective-permute-start(bf16[16,128]{1,0:T(8,128)(2,1)S(1)} %get-tuple-element.20), channel_id=1, source_target_pairs={{0,24},{8,0},{16,8},{24,16},{1,25},{9,1},{17,9},{25,17},{2,26},{10... | collective-permute-start | bytes 12296 | tf_op jit(solution)/shard_map/ppermute | solution.py:30
  9.1 24.1 %collective-permute-start.3 = (bf16[16,128]{1,0:T(8,128)(2,1)S(1)}, bf16[16,128]{1,0:T(8,128)(2,1)S(1)}, u32[]{:S(2)}, u32[]{:S(2)}) collective-permute-start(bf16[16,128]{1,0:T(8,128)(2,1)S(1)} %get-tuple-element.21), channel_id=1, source_target_pairs={{0,24},{8,0},{16,8},{24,16},{1,25},{9,1},{17,9},{25,17},{2,26},{10... | collective-permute-start | bytes 12296 | tf_op jit(solution)/shard_map/ppermute | solution.py:30
  12.6 10.7 %all-to-all-start = ((s32[1,4,4]{1,0,2:T(1,128)}), s32[1,4,4]{1,0,2:T(1,128)S(1)}, u32[]{:S(2)}, u32[]{:S(2)}) async-start(s32[1,4,4]{1,0,2:T(1,128)} %copy.62), calls=%async_computation | async-start | bytes 4096 | tf_op jit(solution)/shard_map/all_to_all | solution.py:144
  18.8 53.0 %collective-permute-start.7 = (bf16[256,192]{0,1:T(8,128)(2,1)S(1)}, bf16[256,192]{0,1:T(8,128)(2,1)S(1)}, u32[]{:S(2)}, u32[]{:S(2)}) collective-permute-start(bf16[256,192]{0,1:T(8,128)(2,1)S(1)} %slice_select_fusion), channel_id=1, source_target_pairs={{0,8},{8,16},{16,24},{24,0},{1,9},{9,17},{17,25},{25,1},{2,10},{10... | collective-permute-start | bytes 294920 | tf_op jit(solution)/shard_map/ppermute | solution.py:30
  26.0 49.0 %all-to-all-start.1 = ((bf16[1,4,4,64,192]{4,3,1,0,2:T(8,128)(2,1)}), bf16[1,4,4,64,192]{4,3,1,0,2:T(8,128)(2,1)S(1)}, u32[]{:S(2)}, u32[]{:S(2)}) async-start(bf16[1,4,4,64,192]{4,3,1,0,2:T(8,128)(2,1)} %copy_select_fusion), calls=%async_computation.1 | async-start | bytes 1048576 | tf_op jit(solution)/shard_map/all_to_all | solution.py:161
  31.0 42.4 %collective-permute-start.8 = (bf16[256,128]{1,0:T(8,128)(2,1)S(1)}, bf16[256,128]{1,0:T(8,128)(2,1)}, u32[]{:S(2)}, u32[]{:S(2)}) collective-permute-start(bf16[256,128]{1,0:T(8,128)(2,1)S(1)} %slice_select_fusion.1), channel_id=1, source_target_pairs={{0,8},{8,16},{16,24},{24,0},{1,9},{9,17},{17,25},{25,1},{2,10},{10... | collective-permute-start | bytes 196616 | tf_op jit(solution)/shard_map/ppermute | solution.py:30
  33.2 38.2 %collective-permute-start.4 = (bf16[1,4,1,64,128]{4,3,2,1,0:T(8,128)(2,1)S(1)}, bf16[1,4,1,64,128]{4,3,2,1,0:T(8,128)(2,1)S(1)}, u32[]{:S(2)}, u32[]{:S(2)}) collective-permute-start(bf16[1,4,1,64,128]{4,3,2,1,0:T(8,128)(2,1)S(1)} %get-tuple-element.19), channel_id=1, source_target_pairs={{0,24},{8,0},{16,8},{24,16},{1,25},{9,1},{17,9},{25,17},{2,26},{10... | collective-permute-start | bytes 196616 | tf_op jit(solution)/shard_map/ppermute | solution.py:22
  51.4 20.1 %collective-permute-start.5 = (bf16[1,4,1,64,128]{4,3,2,1,0:T(8,128)(2,1)S(1)}, bf16[1,4,1,64,128]{4,3,2,1,0:T(8,128)(2,1)S(1)}, u32[]{:S(2)}, u32[]{:S(2)}) collective-permute-start(bf16[1,4,1,64,128]{4,3,2,1,0:T(8,128)(2,1)S(1)} %get-tuple-element.18), channel_id=1, source_target_pairs={{0,16},{8,24},{16,0},{24,8},{1,17},{9,25},{17,1},{25,9},{2,18},{10... | collective-permute-start | bytes 196616 | tf_op jit(solution)/shard_map/ppermute | solution.py:22
  52.3 19.2 %collective-permute-start.6 = (bf16[1,4,1,64,128]{4,3,2,1,0:T(8,128)(2,1)S(1)}, bf16[1,4,1,64,128]{4,3,2,1,0:T(8,128)(2,1)S(1)}, u32[]{:S(2)}, u32[]{:S(2)}) collective-permute-start(bf16[1,4,1,64,128]{4,3,2,1,0:T(8,128)(2,1)S(1)} %get-tuple-element.17), channel_id=1, source_target_pairs={{0,8},{8,16},{16,24},{24,0},{1,9},{9,17},{17,25},{25,1},{2,10},{10... | collective-permute-start | bytes 196616 | tf_op jit(solution)/shard_map/ppermute | solution.py:22
  71.3 0.9 %copy-start.2 = (bf16[512,192]{0,1:T(8,128)(2,1)S(1)}, bf16[512,192]{0,1:T(8,128)(2,1)}, u32[]{:S(2)}) copy-start(bf16[512,192]{0,1:T(8,128)(2,1)} %param.15) | copy-start | bytes 589828
